TPU v7x, 32 devices: a whole 2x2x4 slice. The times are simulated.
32 devices in a mesh: dp: 8 (over z, y), mp: 4 (over x, core).
Axes of the slice: x: 2, y: 2, z: 4, core: 2. Of those that a mesh axis runs over, the one named last changes fastest.
Arguments:
- tokens: bfloat16 [128, 8192], P('dp', 'mp'), may hold values from -6 to 6
- gate_weight: bfloat16 [8192, 21504], P('mp', 'dp'), may hold values from -0.0625 to 0.0625
- up_weight: bfloat16 [8192, 21504], P('mp', 'dp'), may hold values from -0.0625 to 0.0625
- down_weight: bfloat16 [21504, 8192], P('dp', 'mp'), may hold values from -0.0390625 to 0.0390625
Outputs:
- mixed_out: bfloat16 [128, 8192], P('dp', 'mp')
All inputs are finite; a program needn't handle non-finite values.
Results may differ from a plain program's by a relative error of at most 0.005.
Values may be sent and summed in bfloat16 or wider, within the bound.
A program may use at most 128 MiB of HBM per device.

v0:
```python
import jax
import jax.numpy as jnp
from jax import lax
from jax.sharding import PartitionSpec as P


def swiglu(sums):
    return (jax.nn.silu(sums[:, 0, :]) * sums[:, 1, :]).astype(jnp.bfloat16)


def shards(tokens, gate_weight, up_weight, down_weight):
    paired = jnp.stack((gate_weight, up_weight), axis=1)
    partial_sums = jnp.einsum(
        "td,dkf->tkf",
        lax.all_gather(tokens, "dp", axis=0, tiled=True),
        paired,
        preferred_element_type=jnp.float32,
    )
    totals = lax.psum(partial_sums, "mp")
    hidden = swiglu(totals)
    mixed_out = lax.psum_scatter(
        jnp.dot(hidden, down_weight, preferred_element_type=jnp.float32),
        "dp",
        scatter_dimension=0,
        tiled=True,
    )
    return mixed_out.astype(jnp.bfloat16)


def solution(mesh):
    return jax.shard_map(
        shards,
        mesh=mesh,
        in_specs=(P("dp", "mp"), P("mp", "dp"), P("mp", "dp"), P("dp", "mp")),
        out_specs=P("dp", "mp"),
        check_vma=False,
    )
```

profile of v0, /device:TPU:0, one launch (start us, length us, event | category | flops | bytes accessed | tf_op | source)
XLA Modules:
  0.0 223.8 jit_solution(7592698520532821649)
XLA Ops:
  6.5 0.0 all-reduce.2.cloned.1.call-start
  6.5 33.2 %all_gather.3 = bf16[128,2048]{1,0:T(8,128)(2,1)S(1)} all-gather(bf16[16,2048]{1,0:T(8,128)(2,1)} %param.4), channel_id=1, replica_groups=mesh['dp'=8,'mp'=4] {'dp'}, dimensions={0}, use_global_device_ids=true | all-gather | bytes 589824 | tf_op jit(solution)/shard_map/all_gather | solution.py:15
  39.7 14.7 %copy.5 = bf16[2048,2688]{0,1:T(8,128)(2,1)} copy(bf16[2048,2688]{1,0:T(8,128)(2,1)} %param.5) | data formatting | bytes 22020096 | tf_op args[1]
  54.5 14.7 %copy.6 = bf16[2048,2688]{0,1:T(8,128)(2,1)} copy(bf16[2048,2688]{1,0:T(8,128)(2,1)} %param.6) | data formatting | bytes 22020096 | tf_op args[2]
  69.2 11.4 %fusion.4 = f32[128,2,2688]{0,2,1:T(8,128)} fusion(bf16[2048,1,2688]{0,2,1:T(8,128)(2,1)} %bitcast.21, bf16[2048,1,2688]{0,2,1:T(8,128)(2,1)} %bitcast.20, bf16[128,2048]{1,0:T(8,128)(2,1)S(1)} %all_gather.3), kind=kOutput, calls=%fused_computation.4 | convolution fusion | flops 2829582336 | bytes 25296896 | tf_op jit(solution)/shard_map/td,dkf->tkf/dot_general | solution.py:13
  80.7 0.0 all-reduce.2.cloned.1.call-update
  80.7 0.0 reduce-scatter.2.cloned.1.call-start
  80.7 63.3 %all-reduce.2.cloned.1.call-done = f32[128,2,2688]{0,2,1:T(8,128)} async-done(((f32[128,2,2688]{0,2,1:T(8,128)}), f32[128,2,2688]{0,2,1:T(8,128)}) %all-reduce.2.cloned.1.call-update) | async-done | bytes 2752528 | tf_op jit(solution)/shard_map/psum | solution.py:19
  144.0 7.7 %fusion.9 = f32[128,2048]{1,0:T(8,128)} fusion(bf16[2688,2048]{1,0:T(8,128)(2,1)} %param.7, f32[128,2,2688]{0,2,1:T(8,128)} %all-reduce.2.cloned.1.call-done), kind=kOutput, calls=%fused_computation.9 | convolution fusion | flops 1411350528 | bytes 14811136 | tf_op jit(solution)/shard_map/dot_general | solution.py:22
  151.7 0.0 reduce-scatter.2.cloned.1.call-update
  151.7 63.8 %reduce-scatter.2.cloned.1.call-done = f32[16,2048]{1,0:T(8,128)} async-done(((f32[128,2048]{1,0:T(8,128)}), f32[16,2048]{1,0:T(8,128)}) %reduce-scatter.2.cloned.1.call-update) | async-done | bytes 131088 | tf_op jit(solution)/shard_map/reduce_scatter | solution.py:21
  215.4 1.5 convert_element_type.7
Async XLA Ops:
  6.5 137.5 %all-reduce.2.cloned.1.call-start = ((), (), s32[]{:S(2)}) async-start(), calls=%async_computation.1 | async-start | bytes 5505024 | tf_op jit(solution)/shard_map/psum | solution.py:19
  80.7 134.8 %reduce-scatter.2.cloned.1.call-start = ((), (), s32[]{:S(2)}) async-start(), calls=%async_computation.2 | async-start | bytes 1179648 | tf_op jit(solution)/shard_map/reduce_scatter | solution.py:21
Sparse Core Ops, SparseCore 0:
  80.8 63.1 all-reduce.1
  151.8 63.5 reduce-scatter.1
where the time goes:
time: 225 us; the launch traced here: 224 us
  waiting for transfers between devices  127 us (56%)
  blocking collectives  33.2 us (15%)
  local copies, waits for them, and re-layouts  29.5 us (13%)
  matrix products  19.1 us (8%)
  between operations  13.4 us (6%)
    reduce_scatter x1, waiting for transfers between devices, shards(): lax.psum_scatter(jnp.dot(hidden, down_weight, preferred_element_type=jnp....  63.8 us
    psum x1, waiting for transfers between devices, shards(): totals = lax.psum(partial_sums, 'mp')  63.3 us
    all_gather x1, blocking collectives, shards(): lax.all_gather(tokens, 'dp', axis=0, tiled=True)  33.2 us
    unnamed x2, local copies, waits for them, and re-layouts  29.5 us
    dot_general x1, matrix products, shards(): jnp.einsum('td,dkf->tkf', lax.all_gather(tokens, 'dp', axis=0, tiled=True...  11.4 us
    dot_general x1, matrix products, shards(): jnp.dot(hidden, down_weight, preferred_element_type=jnp.float32)  7.67 us
  transfers between devices with their start and end apart: 2, of which 2 were waited for; matrix products, arithmetic and copies ran while one was open for 0% of the time, Pallas kernels for 0%

commit v1 on v0

v1 whole, which is shorter than its diff:
```python
import functools

import jax
import jax.numpy as jnp
from jax import lax
from jax.experimental import pallas as pl
from jax.experimental.pallas import tpu as pltpu
from jax.sharding import PartitionSpec as P

MESH = pl.DeviceIdType.MESH
F32, BF16 = jnp.float32, jnp.bfloat16


def cuts(extent, size):
    out, at = [], 0
    while at < extent:
        out.append((at, min(size, extent - at)))
        at += size
    return out


def tiles(extent):
    step = 256 if extent % 256 == 0 else extent
    return extent // step, step


class Copies:
    def __init__(self):
        self.sent = []

    def start(self, src, dst, send_sem, recv_sem, device):
        copy = pltpu.make_async_remote_copy(
            src_ref=src, dst_ref=dst, send_sem=send_sem, recv_sem=recv_sem,
            device_id=device, device_id_type=MESH,
        )
        copy.start()
        self.sent.append(copy)


def arrived(dst, send_sem, recv_sem, device):
    pltpu.make_async_remote_copy(
        src_ref=dst, dst_ref=dst, send_sem=send_sem, recv_sem=recv_sem,
        device_id=device, device_id_type=MESH,
    ).wait_recv()


def kernel(Z, R, ff_cuts, out_cuts, tok_hbm, gate_hbm, up_hbm, down_hbm, out_ref, s):
    dp, mp = lax.axis_index("dp"), lax.axis_index("mp")
    z, y = lax.div(dp, 2), lax.rem(dp, 2)
    x, core = lax.div(mp, 2), lax.rem(mp, 2)
    C = len(ff_cuts)

    def zdev(d):
        return (lax.rem(z + d, Z) * 2 + y, mp)

    def xdev(d):
        return (dp, lax.rem(x + d, R) * 2 + core)

    ydev = (z * 2 + 1 - y, mp)
    sib = (dp, x * 2 + 1 - core)

    own = pltpu.make_async_copy(tok_hbm, s["tok"].at[z, y], s["own_sem"])
    own.start()
    loads = []
    for c, (at, n) in enumerate(ff_cuts):
        pair = [
            pltpu.make_async_copy(w.at[:, pl.ds(at, n)], s["wgu"][c].at[g], s["w_sem"].at[g, c])
            for g, w in enumerate((gate_hbm, up_hbm))
        ]
        for p in pair:
            p.start()
        loads.append(pair)
    downs = []
    for c, (at, n) in enumerate(ff_cuts):
        p = pltpu.make_async_copy(down_hbm.at[pl.ds(at, n)], s["wd"][c], s["w_sem"].at[2, c])
        p.start()
        downs.append(p)

    barrier = pltpu.get_barrier_semaphore()
    peers = [ydev, sib] + [zdev(d) for d in range(1, Z)] + [xdev(d) for d in range(1, R)]
    for peer in peers:
        pl.semaphore_signal(barrier, inc=1, device_id=peer, device_id_type=MESH)
    pl.semaphore_wait(barrier, len(peers))

    copies = Copies()
    tok = s["tok"]

    for d in range(1, Z):
        copies.start(tok_hbm, tok.at[z, y], s["tz_sem"].at[0, d], s["tz_sem"].at[1, d], zdev(d))
    copies.start(tok_hbm, tok.at[z, y], s["ty_sem"].at[0, 0], s["ty_sem"].at[1, 0], ydev)
    for d in range(1, Z):
        block = tok.at[lax.rem(z + Z - d, Z), y]
        arrived(block, s["tz_sem"].at[0, d], s["tz_sem"].at[1, d], zdev(d))
        copies.start(block, block, s["ty_sem"].at[0, d], s["ty_sem"].at[1, d], ydev)
    for d in range(Z):
        block = tok.at[lax.rem(z + Z - d, Z), 1 - y]
        arrived(block, s["ty_sem"].at[0, d], s["ty_sem"].at[1, d], ydev)
    own.wait()

    rows = tok.shape[0] * 2 * tok.shape[2]
    width = tok.shape[3]
    q = rows // (2 * R)

    def project(c):
        n = ff_cuts[c][1]
        count, step = tiles(n)
        part, w = s["part"][c], s["wgu"][c]
        for g in range(2):
            loads[c][g].wait()

        def body(j, _):
            cols = pl.ds(pl.multiple_of(j * step, 128), step) if count > 1 else slice(None)
            for g in range(2):
                p = jnp.dot(
                    tok[...].reshape(rows, width), w[g, :, cols], preferred_element_type=F32
                ).reshape(R, 2, q, step)
                for k in range(2):
                    part[k, g, :, :, cols] = p[:, k]
            return 0

        if count > 1:
            lax.fori_loop(0, count, body, 0)
        else:
            body(0, 0)
        copies.start(
            part.at[1 - core], s["rx1"][c], s["s1_sem"].at[0, c], s["s1_sem"].at[1, c], sib
        )

    def share(c):
        part, rx1 = s["part"][c], s["rx1"][c]
        arrived(rx1, s["s1_sem"].at[0, c], s["s1_sem"].at[1, c], sib)
        for d in range(1, R):
            r = lax.rem(x + d, R)
            for g in range(2):
                s["tx2"][c][d - 1, g] = (part[core, g, r] + rx1[g, r]).astype(BF16)
            copies.start(
                s["tx2"][c].at[d - 1], s["rx2"][c].at[d - 1],
                s["s2_sem"].at[0, c, d], s["s2_sem"].at[1, c, d], xdev(d),
            )

    def activate(c):
        part, rx1, rx2, hid = s["part"][c], s["rx1"][c], s["rx2"][c], s["hid"][c]
        for d in range(1, R):
            arrived(rx2.at[d - 1], s["s2_sem"].at[0, c, d], s["s2_sem"].at[1, c, d], xdev(d))
        sums = []
        for g in range(2):
            v = part[core, g, x] + rx1[g, x]
            for d in range(1, R):
                v = v + rx2[d - 1, g].astype(F32)
            sums.append(v)
        gate, up = sums
        hid[x, core] = (gate / (1.0 + jnp.exp(-gate)) * up).astype(BF16)
        block = hid.at[x, core]
        for d in range(1, R):
            copies.start(
                block, block, s["s3_sem"].at[0, c, d], s["s3_sem"].at[1, c, d], xdev(d)
            )
        copies.start(block, block, s["s4_sem"].at[0, c, 0], s["s4_sem"].at[1, c, 0], sib)

    def forward(c):
        hid = s["hid"][c]
        for d in range(1, R):
            block = hid.at[lax.rem(x + R - d, R), core]
            arrived(block, s["s3_sem"].at[0, c, d], s["s3_sem"].at[1, c, d], xdev(d))
            copies.start(block, block, s["s4_sem"].at[0, c, d], s["s4_sem"].at[1, c, d], sib)

    acc = s["acc"]

    def mix(c, first, last):
        n = ff_cuts[c][1]
        hid, wd = s["hid"][c], s["wd"][c]
        for d in range(R):
            block = hid.at[lax.rem(x + R - d, R), 1 - core]
            arrived(block, s["s4_sem"].at[0, c, d], s["s4_sem"].at[1, c, d], sib)
        downs[c].wait()
        for j, (at, m) in enumerate(out_cuts):
            count, step = tiles(m)

            def body(i, _):
                cols = pl.ds(pl.multiple_of(at + i * step, 128), step)
                p = jnp.dot(
                    hid[...].reshape(rows, n), wd[:, cols], preferred_element_type=F32
                ).reshape(Z, 2, rows // (2 * Z), step)
                if not first:
                    p = p + acc[:, :, :, cols]
                acc[:, :, :, cols] = p
                return 0

            lax.fori_loop(0, count, body, 0)
            if last:
                ysend(j)

    def ysend(j):
        at, m = out_cuts[j]
        for k in range(Z):
            s["ty"][j][k] = acc[k, 1 - y, :, at:at + m].astype(BF16)
        copies.start(s["ty"][j], s["ry"][j], s["y_sem"].at[0, j], s["y_sem"].at[1, j], ydev)

    def zsend(j):
        at, m = out_cuts[j]
        ry = s["ry"][j]
        arrived(ry, s["y_sem"].at[0, j], s["y_sem"].at[1, j], ydev)
        for d in range(1, Z):
            k = lax.rem(z + d, Z)
            s["tz"][j][d - 1] = (acc[k, y, :, at:at + m] + ry[k].astype(F32)).astype(BF16)
            copies.start(
                s["tz"][j].at[d - 1], s["rz"][j].at[d - 1],
                s["z_sem"].at[0, j, d], s["z_sem"].at[1, j, d], zdev(d),
            )

    def finish(j):
        at, m = out_cuts[j]
        rz = s["rz"][j]
        v = acc[z, y, :, at:at + m] + s["ry"][j][z].astype(F32)
        for d in range(1, Z):
            arrived(rz.at[d - 1], s["z_sem"].at[0, j, d], s["z_sem"].at[1, j, d], zdev(d))
            v = v + rz[d - 1].astype(F32)
        out_ref[:, at:at + m] = v.astype(BF16)

    for c in range(C):
        project(c)
        if c:
            share(c - 1)
    if C > 1:
        activate(0)
    share(C - 1)
    for c in range(min(C, 1), C):
        activate(c)
        if c:
            forward(c - 1)
        if c > 1:
            mix(c - 2, c == 2, False)
    if C == 1:
        activate(0)
    forward(C - 1)
    if C > 1:
        mix(C - 2, C == 2, False)
    mix(C - 1, C == 1, True)
    for j in range(len(out_cuts)):
        zsend(j)
    for j in range(len(out_cuts)):
        finish(j)
    for copy in copies.sent:
        copy.wait_send()


def shards(ndp, nmp, tokens, gate_weight, up_weight, down_weight):
    Z, R = ndp // 2, nmp // 2
    t, width = tokens.shape
    hidden, features = down_weight.shape
    ff_cuts, out_cuts = cuts(hidden, 512), cuts(features, 512)
    C, J = len(ff_cuts), len(out_cuts)
    q = t * ndp // nmp
    dma = pltpu.SemaphoreType.DMA
    V = pltpu.VMEM
    scratch = {
        "tok": V((Z, 2, t, width), BF16),
        "wgu": [V((2, width, n), BF16) for _, n in ff_cuts],
        "wd": [V((n, features), BF16) for _, n in ff_cuts],
        "part": [V((2, 2, R, q, n), F32) for _, n in ff_cuts],
        "rx1": [V((2, R, q, n), F32) for _, n in ff_cuts],
        "tx2": [V((R - 1, 2, q, n), BF16) for _, n in ff_cuts],
        "rx2": [V((R - 1, 2, q, n), BF16) for _, n in ff_cuts],
        "hid": [V((R, 2, q, n), BF16) for _, n in ff_cuts],
        "acc": V((Z, 2, t, features), F32),
        "ty": [V((Z, t, m), BF16) for _, m in out_cuts],
        "ry": [V((Z, t, m), BF16) for _, m in out_cuts],
        "tz": [V((Z - 1, t, m), BF16) for _, m in out_cuts],
        "rz": [V((Z - 1, t, m), BF16) for _, m in out_cuts],
        "own_sem": dma,
        "w_sem": dma((3, C)),
        "tz_sem": dma((2, Z)),
        "ty_sem": dma((2, Z)),
        "s1_sem": dma((2, C)),
        "s2_sem": dma((2, C, R)),
        "s3_sem": dma((2, C, R)),
        "s4_sem": dma((2, C, R)),
        "y_sem": dma((2, J)),
        "z_sem": dma((2, J, Z)),
    }
    leaves, tree = jax.tree.flatten(scratch)

    def body(*refs):
        kernel(Z, R, ff_cuts, out_cuts, *refs[:5], jax.tree.unflatten(tree, refs[5:]))

    flops = 6 * t * ndp * width * hidden
    return pl.pallas_call(
        body,
        out_shape=jax.ShapeDtypeStruct((t, features), BF16),
        in_specs=[pl.BlockSpec(memory_space=pl.ANY)] * 4,
        out_specs=pl.BlockSpec(memory_space=pltpu.VMEM),
        scratch_shapes=leaves,
        compiler_params=pltpu.CompilerParams(
            collective_id=0, has_side_effects=True, vmem_limit_bytes=58 * 2**20
        ),
        cost_estimate=pl.CostEstimate(
            flops=flops, bytes_accessed=6 * width * hidden, transcendentals=0
        ),
        name="ffn",
    )(tokens, gate_weight, up_weight, down_weight)


def solution(mesh):
    return jax.shard_map(
        functools.partial(shards, mesh.shape["dp"], mesh.shape["mp"]),
        mesh=mesh,
        in_specs=(P("dp", "mp"), P("mp", "dp"), P("mp", "dp"), P("dp", "mp")),
        out_specs=P("dp", "mp"),
        check_vma=False,
    )
```

time: 225 us -> 55.1 us (0.24)
  waiting for transfers between devices: 127 us -> 0 us
  Pallas kernels: 0 us -> 53.4 us
  blocking collectives: 33.2 us -> 0 us
  local copies, waits for them, and re-layouts: 29.5 us -> 1.47 us
  matrix products: 19.1 us -> 0 us
  between operations: 13.4 us -> 0.01 us
    reduce_scatter x1 -> x0, waiting for transfers between devices: 63.8 us -> none  [shards(): lax.psum_scatter(jnp.dot(hidden, down_weight, preferred_element_type=jnp....]
    psum x1 -> x0, waiting for transfers between devices: 63.3 us -> none  [shards(): totals = lax.psum(partial_sums, 'mp')]
    pallas_call x0 -> x1, Pallas kernels: none -> 53.4 us  [shards(): pl.pallas_call(body, out_shape=jax.ShapeDtypeStruct((t, features), BF16),...]
    all_gather x1 -> x0, blocking collectives: 33.2 us -> none  [shards(): lax.all_gather(tokens, 'dp', axis=0, tiled=True)]
    unnamed x2 -> x1, local copies, waits for them, and re-layouts: 29.5 us -> 1.47 us
    dot_general x2 -> x0, matrix products: 19.1 us -> none  [the longest x1 11.4 us: shards(): jnp.einsum('td,dkf->tkf', lax.all_gather(tokens, 'dp', axis=0, tiled=True...]
  transfers between devices with their start and end apart: 2 -> 0, of which waited for: 2 -> 0; matrix products, arithmetic and copies ran while one was open for 0% -> 0% of each run, Pallas kernels for 0% -> 0%
where the time goes in v1:
time: 55.1 us; the launch traced here: 54.9 us
  Pallas kernels  53.4 us (97%)
  local copies, waits for them, and re-layouts  1.47 us (3%)
    pallas_call x1, Pallas kernels, shards(): pl.pallas_call(body, out_shape=jax.ShapeDtypeStruct((t, features), BF16),...  53.4 us
    unnamed x1, local copies, waits for them, and re-layouts  1.47 us

profile of v1, /device:TPU:0, one launch (start us, length us, event | category | flops | bytes accessed | tf_op | source)
XLA Modules:
  0.0 54.9 jit_solution(6454100935501610814)
XLA Ops:
  0.0 53.4 %ffn.1 = bf16[16,2048]{1,0:T(8,128)(2,1)} custom-call(bf16[16,2048]{1,0:T(8,128)(2,1)} %refs_0_.1, bf16[2048,2688]{1,0:T(8,128)(2,1)} %refs_1_.1, bf16[2048,2688]{1,0:T(8,128)(2,1)} %refs_2_.1, bf16[2688,2048]{1,0:T(8,128)(2,1)} %refs_3_.1), custom_call_target="tpu_custom_call" | custom-call | flops 4227858432 | bytes 33030144 | tf_op jit(solution)/shard_map/ffn/pallas_call | solution.py:287
  53.4 1.5 %copy.6 = bf16[16,2048]{1,0:T(8,128)(2,1)} copy(bf16[16,2048]{1,0:T(8,128)(2,1)} %ffn.1) | data formatting | bytes 131072

commit v2 on v1

v2 whole, which is shorter than its diff:
```python
import functools

import jax
import jax.numpy as jnp
from jax import lax
from jax.experimental import pallas as pl
from jax.experimental.pallas import tpu as pltpu
from jax.sharding import PartitionSpec as P

MESH = pl.DeviceIdType.MESH
F32, BF16 = jnp.float32, jnp.bfloat16


def cuts(extent, size):
    out, at = [], 0
    while at < extent:
        out.append((at, min(size, extent - at)))
        at += size
    return out


def tiles(extent):
    step = next((k for k in (768, 512, 384, 256) if extent % k == 0), extent)
    return extent // step, step


class Copies:
    def __init__(self):
        self.sent = []

    def make(self, src, dst, send_sem, recv_sem, device):
        copy = pltpu.make_async_remote_copy(
            src_ref=src, dst_ref=dst, send_sem=send_sem, recv_sem=recv_sem,
            device_id=device, device_id_type=MESH,
        )
        self.sent.append(copy)
        return copy

    def start(self, *args):
        self.make(*args).start()


def arrived(dst, send_sem, recv_sem, device):
    pltpu.make_async_remote_copy(
        src_ref=dst, dst_ref=dst, send_sem=send_sem, recv_sem=recv_sem,
        device_id=device, device_id_type=MESH,
    ).wait_recv()


def kernel(Z, R, ff_cuts, out_cuts, tok_hbm, gate_hbm, up_hbm, down_hbm, out_ref, s):
    dp, mp = lax.axis_index("dp"), lax.axis_index("mp")
    z, y = lax.div(dp, 2), lax.rem(dp, 2)
    x, core = lax.div(mp, 2), lax.rem(mp, 2)
    C = len(ff_cuts)

    def zdev(d):
        return (lax.rem(z + d, Z) * 2 + y, mp)

    def xdev(d):
        return (dp, lax.rem(x + d, R) * 2 + core)

    ydev = (z * 2 + 1 - y, mp)
    sib = (dp, x * 2 + 1 - core)

    tok, H = s["tok"], Z // 2
    h0, z2 = lax.rem(z + y, 2), lax.div(z, 2)

    def at_distance(h, i, across):
        yy = 1 - y if across else y
        k = 2 * i + lax.rem(yy + h, 2)
        return k, lax.rem(z + Z - k, Z)

    own = pltpu.make_async_copy(tok_hbm, tok.at[h0, z2, y], s["own_sem"])
    own.start()
    loads = []
    for c, (at, n) in enumerate(ff_cuts):
        pair = [
            pltpu.make_async_copy(w.at[:, pl.ds(at, n)], s["wgu"][c].at[g], s["w_sem"].at[g, c])
            for g, w in enumerate((gate_hbm, up_hbm))
        ]
        for p in pair:
            p.start()
        loads.append(pair)
    downs = []
    for c, (at, n) in enumerate(ff_cuts):
        p = pltpu.make_async_copy(down_hbm.at[pl.ds(at, n)], s["wd"][c], s["w_sem"].at[2, c])
        p.start()
        downs.append(p)

    barrier = pltpu.get_barrier_semaphore()
    peers = [ydev, sib] + [zdev(d) for d in range(1, Z)] + [xdev(d) for d in range(1, R)]
    for peer in peers:
        pl.semaphore_signal(barrier, inc=1, device_id=peer, device_id_type=MESH)
    pl.semaphore_wait(barrier, len(peers))

    copies = Copies()

    mine = tok.at[h0, z2, y]
    first = [
        copies.make(tok_hbm, mine, s["tz_sem"].at[0, d], s["tz_sem"].at[1, d], zdev(d))
        for d in range(1, Z)
    ]
    first.append(
        copies.make(tok_hbm, mine, s["ty_sem"].at[0, 0], s["ty_sem"].at[1, 0], ydev)
    )

    def send_own(h):
        @pl.when(h0 == h)
        def _():
            for copy in first:
                copy.start()

    def pass_on(h):
        for i in range(H):
            _, d = at_distance(h, i, False)

            @pl.when(d > 0)
            def _():
                block = tok.at[h, i, y]
                arrived(block, s["tz_sem"].at[0, d], s["tz_sem"].at[1, d], zdev(1))
                pltpu.make_async_remote_copy(
                    src_ref=block, dst_ref=block, send_sem=s["ty_sem"].at[0, d],
                    recv_sem=s["ty_sem"].at[1, d], device_id=ydev, device_id_type=MESH,
                ).start()

    def gathered(h):
        for i in range(H):
            _, d = at_distance(h, i, True)
            arrived(
                tok.at[h, i, 1 - y], s["ty_sem"].at[0, d], s["ty_sem"].at[1, d], ydev
            )

    rows = tok.shape[1] * 2 * tok.shape[3]
    width = tok.shape[4]
    q = rows // (2 * R)

    def project(h, c):
        n = ff_cuts[c][1]
        count, step = tiles(n)
        part, w = s["part"][h][c], s["wgu"][c]
        if h == 0:
            for g in range(2):
                loads[c][g].wait()

        def body(j, _):
            cols = pl.ds(pl.multiple_of(j * step, 128), step) if count > 1 else slice(None)
            for g in range(2):
                p = jnp.dot(
                    tok[h].reshape(rows, width), w[g, :, cols], preferred_element_type=F32
                ).reshape(R, 2, q, step)
                for k in range(2):
                    part[k, g, :, :, cols] = p[:, k]
            return 0

        if count > 1:
            lax.fori_loop(0, count, body, 0)
        else:
            body(0, 0)
        copies.start(
            part.at[1 - core], s["rx1"][h][c], s["s1_sem"].at[0, h, c], s["s1_sem"].at[1, h, c], sib
        )

    def share(h, c):
        part, rx1 = s["part"][h][c], s["rx1"][h][c]
        arrived(rx1, s["s1_sem"].at[0, h, c], s["s1_sem"].at[1, h, c], sib)
        for d in range(1, R):
            r = lax.rem(x + d, R)
            for g in range(2):
                s["tx2"][h][c][d - 1, g] = (part[core, g, r] + rx1[g, r]).astype(BF16)
            copies.start(
                s["tx2"][h][c].at[d - 1], s["rx2"][h][c].at[d - 1],
                s["s2_sem"].at[0, h, c, d], s["s2_sem"].at[1, h, c, d], xdev(d),
            )

    def activate(h, c):
        part, rx1, rx2, hid = s["part"][h][c], s["rx1"][h][c], s["rx2"][h][c], s["hid"][h][c]
        for d in range(1, R):
            arrived(rx2.at[d - 1], s["s2_sem"].at[0, h, c, d], s["s2_sem"].at[1, h, c, d], xdev(d))
        sums = []
        for g in range(2):
            v = part[core, g, x] + rx1[g, x]
            for d in range(1, R):
                v = v + rx2[d - 1, g].astype(F32)
            sums.append(v)
        gate, up = sums
        hid[x, core] = (gate / (1.0 + jnp.exp(-gate)) * up).astype(BF16)
        block = hid.at[x, core]
        for d in range(1, R):
            copies.start(
                block, block, s["s3_sem"].at[0, h, c, d], s["s3_sem"].at[1, h, c, d], xdev(d)
            )
        copies.start(block, block, s["s4_sem"].at[0, h, c, 0], s["s4_sem"].at[1, h, c, 0], sib)

    def forward(h, c):
        hid = s["hid"][h][c]
        for d in range(1, R):
            block = hid.at[lax.rem(x + R - d, R), core]
            arrived(block, s["s3_sem"].at[0, h, c, d], s["s3_sem"].at[1, h, c, d], xdev(d))
            copies.start(block, block, s["s4_sem"].at[0, h, c, d], s["s4_sem"].at[1, h, c, d], sib)

    acc = s["acc"]

    def mix(h, c, first, last):
        n = ff_cuts[c][1]
        hid, wd = s["hid"][h][c], s["wd"][c]
        for d in range(R):
            block = hid.at[lax.rem(x + R - d, R), 1 - core]
            arrived(block, s["s4_sem"].at[0, h, c, d], s["s4_sem"].at[1, h, c, d], sib)
        if h == 0:
            downs[c].wait()
        for j, (at, m) in enumerate(out_cuts):
            count, step = tiles(m)

            def body(i, _):
                cols = pl.ds(pl.multiple_of(at + i * step, 128), step)
                p = jnp.dot(
                    hid[...].reshape(rows, n), wd[:, cols], preferred_element_type=F32
                ).reshape(H, 2, rows // Z, step)
                if not first:
                    p = p + acc[h, :, :, :, cols]
                acc[h, :, :, :, cols] = p
                return 0

            lax.fori_loop(0, count, body, 0)
            if last:
                ysend(h, j)

    def ysend(h, j):
        at, m = out_cuts[j]
        ty, ry = s["ty"][j].at[h], s["ry"][j].at[h]
        for i in range(H):
            ty[i] = acc[h, i, 1 - y, :, at:at + m].astype(BF16)
        copies.start(ty, ry, s["y_sem"].at[0, h, j], s["y_sem"].at[1, h, j], ydev)

    def zsend(h, j):
        at, m = out_cuts[j]
        ry, tz, rz = s["ry"][j].at[h], s["tz"][j], s["rz"][j]
        arrived(ry, s["y_sem"].at[0, h, j], s["y_sem"].at[1, h, j], ydev)
        for i in range(H):
            k = 2 * i + lax.rem(y + h, 2)
            d = lax.rem(k + Z - z, Z)

            @pl.when(d > 0)
            def _():
                tz[d - 1] = (acc[h, i, y, :, at:at + m] + ry[i].astype(F32)).astype(BF16)
                pltpu.make_async_remote_copy(
                    src_ref=tz.at[d - 1], dst_ref=rz.at[d - 1],
                    send_sem=s["z_sem"].at[0, j, d], recv_sem=s["z_sem"].at[1, j, d],
                    device_id=zdev(d), device_id_type=MESH,
                ).start()

    def finish(j):
        at, m = out_cuts[j]
        rz = s["rz"][j]
        v = acc[h0, z2, y, :, at:at + m] + s["ry"][j][h0, z2].astype(F32)
        for d in range(1, Z):
            arrived(rz.at[d - 1], s["z_sem"].at[0, j, d], s["z_sem"].at[1, j, d], zdev(d))
            v = v + rz[d - 1].astype(F32)
        out_ref[:, at:at + m] = v.astype(BF16)

    J = len(out_cuts)
    send_own(0)
    send_own(1)
    pass_on(0)
    pass_on(1)
    own.wait()
    gathered(0)
    for c in range(C):
        project(0, c)
        if c:
            share(0, c - 1)
    share(0, C - 1)
    gathered(1)
    for c in range(C):
        project(1, c)
        if c:
            share(1, c - 1)
        activate(0, c)
    share(1, C - 1)
    for c in range(C):
        forward(0, c)
    for c in range(C):
        mix(0, c, c == 0, c == C - 1)
        activate(1, c)
    for c in range(C):
        forward(1, c)
        if c:
            mix(1, c - 1, c == 1, False)
    for j in range(J):
        zsend(0, j)
    mix(1, C - 1, C == 1, True)
    for j in range(J):
        zsend(1, j)
    for j in range(J):
        finish(j)
    for copy in copies.sent:
        copy.wait_send()
    for d in range(1, Z):
        pltpu.make_async_remote_copy(
            src_ref=mine, dst_ref=mine, send_sem=s["ty_sem"].at[0, d],
            recv_sem=s["ty_sem"].at[1, d], device_id=ydev, device_id_type=MESH,
        ).wait_send()
        for j in range(J):
            block = s["tz"][j].at[d - 1]
            pltpu.make_async_remote_copy(
                src_ref=block, dst_ref=block, send_sem=s["z_sem"].at[0, j, d],
                recv_sem=s["z_sem"].at[1, j, d], device_id=zdev(d), device_id_type=MESH,
            ).wait_send()


def shards(ndp, nmp, tokens, gate_weight, up_weight, down_weight):
    Z, R = ndp // 2, nmp // 2
    t, width = tokens.shape
    hidden, features = down_weight.shape
    ff_cuts, out_cuts = cuts(hidden, 768), cuts(features, 512)
    C, J = len(ff_cuts), len(out_cuts)
    H, q = Z // 2, t * ndp // (2 * nmp)
    dma = pltpu.SemaphoreType.DMA
    V = pltpu.VMEM
    scratch = {
        "tok": V((2, H, 2, t, width), BF16),
        "wgu": [V((2, width, n), BF16) for _, n in ff_cuts],
        "wd": [V((n, features), BF16) for _, n in ff_cuts],
        "part": [[V((2, 2, R, q, n), F32) for _, n in ff_cuts] for _ in range(2)],
        "rx1": [[V((2, R, q, n), F32) for _, n in ff_cuts] for _ in range(2)],
        "tx2": [[V((R - 1, 2, q, n), BF16) for _, n in ff_cuts] for _ in range(2)],
        "rx2": [[V((R - 1, 2, q, n), BF16) for _, n in ff_cuts] for _ in range(2)],
        "hid": [[V((R, 2, q, n), BF16) for _, n in ff_cuts] for _ in range(2)],
        "acc": V((2, H, 2, t, features), F32),
        "ty": [V((2, H, t, m), BF16) for _, m in out_cuts],
        "ry": [V((2, H, t, m), BF16) for _, m in out_cuts],
        "tz": [V((Z - 1, t, m), BF16) for _, m in out_cuts],
        "rz": [V((Z - 1, t, m), BF16) for _, m in out_cuts],
        "own_sem": dma,
        "w_sem": dma((3, C)),
        "tz_sem": dma((2, Z)),
        "ty_sem": dma((2, Z)),
        "s1_sem": dma((2, 2, C)),
        "s2_sem": dma((2, 2, C, R)),
        "s3_sem": dma((2, 2, C, R)),
        "s4_sem": dma((2, 2, C, R)),
        "y_sem": dma((2, 2, J)),
        "z_sem": dma((2, J, Z)),
    }
    leaves, tree = jax.tree.flatten(scratch)

    def body(*refs):
        kernel(Z, R, ff_cuts, out_cuts, *refs[:5], jax.tree.unflatten(tree, refs[5:]))

    flops = 6 * t * ndp * width * hidden
    return pl.pallas_call(
        body,
        out_shape=jax.ShapeDtypeStruct((t, features), BF16),
        in_specs=[pl.BlockSpec(memory_space=pl.ANY)] * 4,
        out_specs=pl.BlockSpec(memory_space=pltpu.VMEM),
        scratch_shapes=leaves,
        compiler_params=pltpu.CompilerParams(
            collective_id=0, has_side_effects=True, vmem_limit_bytes=58 * 2**20
        ),
        cost_estimate=pl.CostEstimate(
            flops=flops, bytes_accessed=6 * width * hidden, transcendentals=0
        ),
        name="ffn",
    )(tokens, gate_weight, up_weight, down_weight)


def solution(mesh):
    return jax.shard_map(
        functools.partial(shards, mesh.shape["dp"], mesh.shape["mp"]),
        mesh=mesh,
        in_specs=(P("dp", "mp"), P("mp", "dp"), P("mp", "dp"), P("dp", "mp")),
        out_specs=P("dp", "mp"),
        check_vma=False,
    )
```

time: 55.1 us -> 48.1 us (0.87)
  the two profiles are of different devices: /device:TPU:0 before, /device:TPU:6 now
where the time goes in v2:
time: 48.1 us; the launch traced here: 47.9 us
  Pallas kernels  46.4 us (96%)
  local copies, waits for them, and re-layouts  1.47 us (3%)
    pallas_call x1, Pallas kernels, shards(): pl.pallas_call(body, out_shape=jax.ShapeDtypeStruct((t, features), BF16),...  46.4 us
    unnamed x1, local copies, waits for them, and re-layouts  1.47 us

profile of v2, /device:TPU:6, one launch (start us, length us, event | category | flops | bytes accessed | tf_op | source)
XLA Modules:
  0.0 47.9 jit_solution(18343289735997517907)
XLA Ops:
  0.0 46.4 %ffn.1 = bf16[16,2048]{1,0:T(8,128)(2,1)} custom-call(bf16[16,2048]{1,0:T(8,128)(2,1)} %refs_0_.1, bf16[2048,2688]{1,0:T(8,128)(2,1)} %refs_1_.1, bf16[2048,2688]{1,0:T(8,128)(2,1)} %refs_2_.1, bf16[2688,2048]{1,0:T(8,128)(2,1)} %refs_3_.1), custom_call_target="tpu_custom_call" | custom-call | flops 4227858432 | bytes 33030144 | tf_op jit(solution)/shard_map/ffn/pallas_call | solution.py:351
  46.4 1.5 %copy.6 = bf16[16,2048]{1,0:T(8,128)(2,1)} copy(bf16[16,2048]{1,0:T(8,128)(2,1)} %ffn.1) | data formatting | bytes 131072
